TPU v7x, 128 devices: a whole 4x4x4 slice. The times are simulated.
128 devices in a mesh: ab: 32 (over z, x, core), cd: 4 (over y).
Axes of the slice: x: 4, y: 4, z: 4, core: 2. Of those that a mesh axis runs over, the one named last changes fastest.
Arguments:
- amplitudes: bfloat16 [2048, 16384], P('ab', 'cd'), may hold values from -6 to 6
- integrals: bfloat16 [16384, 40960], P('cd', 'ab'), may hold values from -0.125 to 0.125
- ab_sizes: int32 [8], replicated, may hold values from 128 to 20480, as said below
- cd_sizes: int32 [8], replicated, may hold values from 512 to 8192, as said below
- virt_energy: float32 [40960], P('ab'), may hold values from 1 to 4
- occ_energy: float32 [2048], P('cd'), may hold values from -2 to -0.5
Outputs:
- residual: float32 [2048, 40960], P('cd', 'ab')
- update: float32 [2048, 40960], P('cd', 'ab')
Inputs may be any that keep to these rules, and one draw needn't show every extreme that they name: `ab_sizes`: each entry is a positive multiple of 128; the 8 entries sum to 40960. `cd_sizes`: each entry is a positive multiple of 512; the 8 entries sum to 16384.
All inputs are finite; a program needn't handle non-finite values.
Results may differ from a plain program's by a relative error of at most 0.0003.
Values may be sent and summed in bfloat16 or wider, within the bound.
A program may use at most 256 MiB of HBM per device.

v0:
```python
import jax
import jax.numpy as jnp
from jax import lax
from jax.sharding import PartitionSpec as P

TCD = 512


def irrep_of(sizes, positions):
    ends = jnp.cumsum(sizes)
    return jnp.sum((positions[:, None] >= ends[None, :]).astype(jnp.int32), axis=1)


def body(amplitudes, integrals, ab_sizes, cd_sizes, virt_energy, occ_energy):
    cd_local, ab_local = integrals.shape
    ab_start = lax.axis_index("ab") * ab_local
    cd_start = lax.axis_index("cd") * cd_local
    column_irrep = irrep_of(ab_sizes, ab_start + jnp.arange(ab_local, dtype=jnp.int32))
    tile_count = cd_local // TCD
    tile_irrep = irrep_of(cd_sizes, cd_start + jnp.arange(tile_count, dtype=jnp.int32) * TCD)
    rows = lax.all_gather(amplitudes, "ab", axis=0, tiled=True)
    total = jnp.zeros((rows.shape[0], ab_local), jnp.float32)
    for tile in range(tile_count):
        left = rows[:, tile * TCD : (tile + 1) * TCD]
        right = integrals[tile * TCD : (tile + 1) * TCD]
        irrep = tile_irrep[tile]
        product = jnp.dot(left, right, preferred_element_type=jnp.float32)
        total = total + jnp.where(column_irrep[None, :] == irrep, product, jnp.float32(0.0))
    residual = lax.psum_scatter(total, "cd", scatter_dimension=0, tiled=True)
    update = residual / (virt_energy[None, :] - occ_energy[:, None])
    return (residual, update)


def solution(mesh):
    placed = (P("ab", "cd"), P("cd", "ab"), P(), P(), P("ab"), P("cd"))
    return jax.shard_map(
        body, mesh=mesh, in_specs=placed, out_specs=(P("cd", "ab"), P("cd", "ab")), check_vma=False
    )
```

profile of v0, /device:TPU:18, one launch (start us, length us, event | category | flops | bytes accessed | tf_op | source)
XLA Modules:
  0.0 266.7 jit_solution(14760268605523439382)
XLA Ops:
  7.2 0.0 all-gather.2.cloned.1.call-start
  7.2 0.7 all-gather.2.cloned.1.call-update
  7.9 0.0 reduce-scatter.2.cloned.1.call-start
  7.9 0.8 reduce-window.16
  8.8 0.8 reduce-window.17
  9.6 0.2 convert_reduce_fusion.1
  9.8 0.7 fusion.23
  10.5 0.1 convert_reduce_fusion
  10.6 5.0 %broadcast_compare_fusion.7 = (pred[1280]{0:T(1024)(128)(4,1)S(1)}, pred[1280]{0:T(1024)(128)(4,1)S(1)}, pred[1280]{0:T(1024)(128)(4,1)S(1)}, pred[1280]{0:T(102...) fusion(s32[1280]{0:T(1024)S(1)} %convert_reduce_fusion, ...), kind=kLoop, calls=%fused_computation.34 | loop fusion | flops 10240 | bytes 15392 | tf_op jit(solution)/shard_map/eq | solution.py:28
  15.6 69.5 %all-gather.2.cloned.1.call-done = bf16[2048,4096]{1,0:T(8,128)(2,1)} async-done(((bf16[64,4096]{1,0:T(8,128)(2,1)}), bf16[2048,4096]{1,0:T(8,128)(2,1)}) %all-gather.2.cloned.1.call-update) | async-done | bytes 16777232 | tf_op jit(solution)/shard_map/all_gather | solution.py:21
  85.1 0.0 copy-start
  85.1 9.4 %fusion.1 = f32[2048,1280]{1,0:T(8,128)} fusion(bf16[2048,4096]{1,0:T(8,128)(2,1)} %all-gather.2.cloned.1.call-done, bf16[4096,1280]{1,0:T(8,128)(2,1)} %param.7), kind=kOutput, calls=%fused_computation.3 | convolution fusion | flops 2684354560 | bytes 13893632 | tf_op jit(solution)/shard_map/dot_general | solution.py:27
  94.5 0.0 copy-start.1
  94.5 9.0 %fusion.3 = f32[2048,1280]{1,0:T(8,128)} fusion(bf16[2048,4096]{1,0:T(8,128)(2,1)} %all-gather.2.cloned.1.call-done, bf16[4096,1280]{1,0:T(8,128)(2,1)} %param.7), kind=kOutput, calls=%fused_computation.5 | convolution fusion | flops 2684354560 | bytes 13893632 | tf_op jit(solution)/shard_map/dot_general | solution.py:27
  103.5 0.0 copy-done
  103.5 0.0 copy-done.1
  103.5 5.5 %fusion.5 = f32[2048,1280]{1,0:T(8,128)} fusion(bf16[2048,4096]{1,0:T(8,128)(2,1)S(1)} %copy-done, bf16[4096,1280]{1,0:T(8,128)(2,1)S(1)} %copy-done.1), kind=kOutput, calls=%fused_computation.7 | convolution fusion | flops 2684354560 | bytes 13893632 | tf_op jit(solution)/shard_map/dot_general | solution.py:27
  109.0 5.5 %fusion.7 = f32[2048,1280]{1,0:T(8,128)} fusion(bf16[2048,4096]{1,0:T(8,128)(2,1)S(1)} %copy-done, bf16[4096,1280]{1,0:T(8,128)(2,1)S(1)} %copy-done.1), kind=kOutput, calls=%fused_computation.9 | convolution fusion | flops 2684354560 | bytes 13893632 | tf_op jit(solution)/shard_map/dot_general | solution.py:27
  114.5 5.4 %fusion.9 = f32[2048,1280]{1,0:T(8,128)} fusion(bf16[2048,4096]{1,0:T(8,128)(2,1)S(1)} %copy-done, bf16[4096,1280]{1,0:T(8,128)(2,1)S(1)} %copy-done.1), kind=kOutput, calls=%fused_computation.11 | convolution fusion | flops 2684354560 | bytes 13893632 | tf_op jit(solution)/shard_map/dot_general | solution.py:27
  119.9 5.4 %fusion.11 = f32[2048,1280]{1,0:T(8,128)} fusion(bf16[2048,4096]{1,0:T(8,128)(2,1)S(1)} %copy-done, bf16[4096,1280]{1,0:T(8,128)(2,1)S(1)} %copy-done.1), kind=kOutput, calls=%fused_computation.13 | convolution fusion | flops 2684354560 | bytes 13893632 | tf_op jit(solution)/shard_map/dot_general | solution.py:27
  125.3 5.4 %fusion.13 = f32[2048,1280]{1,0:T(8,128)} fusion(bf16[2048,4096]{1,0:T(8,128)(2,1)S(1)} %copy-done, bf16[4096,1280]{1,0:T(8,128)(2,1)S(1)} %copy-done.1), kind=kOutput, calls=%fused_computation.15 | convolution fusion | flops 2684354560 | bytes 13893632 | tf_op jit(solution)/shard_map/dot_general | solution.py:27
  130.6 30.0 %select_add_fusion = f32[2048,1280]{1,0:T(8,128)} fusion(f32[2048,1280]{1,0:T(8,128)} %fusion.1, f32[2048,1280]{1,0:T(8,128)} %fusion.3, f32[2048,1280]{1,0:T(8,128)} %fusion.5, f32[2048,1280]{1,0:T(8,128)} %fusion.7, f32[2048,1280]{1,0:T(8,128)} %fusion.9, f32[2048,1280]{1,0:T(8,128)} %fusion.11, f32[2048,1280]{1,0:T(8,128)} %fusion.13, ...), kind=kOutput, calls=%fused_computation | convolution fusion | flops 2723676160 | bytes 87304192 | tf_op jit(solution)/shard_map/dot_general | solution.py:27
  160.6 0.0 copy-start.2
  160.6 0.0 copy-start.3
  160.6 0.0 reduce-scatter.2.cloned.1.call-update
  160.7 95.5 %reduce-scatter.2.cloned.1.call-done = f32[512,1280]{1,0:T(8,128)} async-done(((f32[2048,1280]{1,0:T(8,128)}), f32[512,1280]{1,0:T(8,128)}) %reduce-scatter.2.cloned.1.call-update) | async-done | bytes 2621456 | tf_op jit(solution)/shard_map/reduce_scatter | solution.py:29
  256.2 0.0 copy-done.2
  256.2 0.0 copy-done.3
  256.2 3.6 %subtract_divide_fusion = f32[512,1280]{1,0:T(8,128)} fusion(f32[512,1280]{1,0:T(8,128)} %reduce-scatter.2.cloned.1.call-done, f32[512]{0:T(512)S(1)} %copy-done.3, f32[1280]{0:T(1024)S(1)} %copy-done.2), kind=kLoop, calls=%fused_computation.1 | loop fusion | flops 1310720 | bytes 5250048 | tf_op jit(solution)/shard_map/div | solution.py:30
  (2 shorter events, 0.0 us)
Async XLA Ops:
  7.2 77.9 %all-gather.2.cloned.1.call-start = ((), (), s32[]{:S(2)}) async-start(), calls=%async_computation.1 | async-start | bytes 17301504 | tf_op jit(solution)/shard_map/all_gather | solution.py:21
  7.9 248.3 %reduce-scatter.2.cloned.1.call-start = ((), (), s32[]{:S(2)}) async-start(), calls=%async_computation.2 | async-start | bytes 13107200 | tf_op jit(solution)/shard_map/reduce_scatter | solution.py:29
  85.1 18.4 %copy-start = (bf16[2048,4096]{1,0:T(8,128)(2,1)S(1)}, bf16[2048,4096]{1,0:T(8,128)(2,1)}, u32[]{:S(2)}) copy-start(bf16[2048,4096]{1,0:T(8,128)(2,1)} %all-gather.2.cloned.1.call-done) | copy-start | bytes 50331652
  94.5 9.0 %copy-start.1 = (bf16[4096,1280]{1,0:T(8,128)(2,1)S(1)}, bf16[4096,1280]{1,0:T(8,128)(2,1)}, u32[]{:S(2)}) copy-start(bf16[4096,1280]{1,0:T(8,128)(2,1)} %param.7) | copy-start | bytes 31457284
  160.6 95.6 %copy-start.2 = (f32[1280]{0:T(1024)S(1)}, f32[1280]{0:T(1024)}, u32[]{:S(2)}) copy-start(f32[1280]{0:T(1024)} %param.10) | copy-start | bytes 15364
  160.6 95.6 %copy-start.3 = (f32[512]{0:T(512)S(1)}, f32[512]{0:T(512)}, u32[]{:S(2)}) copy-start(f32[512]{0:T(512)} %param.11) | copy-start | bytes 6148
Sparse Core Ops, SparseCore 0:
  10.3 74.7 all-gather.1
  160.8 95.3 reduce-scatter.1
where the time goes:
time: 270 us; the launch traced here: 267 us
  waiting for transfers between devices  166 us (61%)
  matrix products  75.5 us (28%)
  between operations  14.1 us (5%)
  other arithmetic  10.6 us (4%)
    reduce_scatter x1, waiting for transfers between devices, body(): residual = lax.psum_scatter(total, 'cd', scatter_dimension=0, tiled=True)  95.5 us
    dot_general x8, matrix products, body(): product = jnp.dot(left, right, preferred_element_type=jnp.float32)  75.5 us
    all_gather x1, waiting for transfers between devices, body(): rows = lax.all_gather(amplitudes, 'ab', axis=0, tiled=True)  69.5 us
  transfers between devices with their start and end apart: 2, of which 2 were waited for; matrix products, arithmetic and copies ran while one was open for 3% of the time, Pallas kernels for 0%

commit v1 on v0

v1 whole, which is shorter than its diff:
```python
import functools

import jax
import jax.numpy as jnp
from jax import lax
from jax.experimental import pallas as pl
from jax.experimental.pallas import tpu as pltpu
from jax.sharding import PartitionSpec as P

MESH = pl.DeviceIdType.MESH
TCD = 512
LANES = 128
TOP = 32000.0
FINE = 64.0

ORDER = (
    (0, 0), (1, 0), (3, 0), (0, 1), (0, 3), (2, 0), (0, 2), (1, 1),
    (1, 3), (1, 2), (3, 1), (3, 3), (3, 2), (2, 1), (2, 3), (2, 2),
)
SLOT = {d: k for k, d in enumerate(ORDER)}
STEPS = len(ORDER)
HANDLE = {1: (1, 2), 2: (3, 4), 4: (5, 6), 6: (7, 8), 8: (9,), 9: (10, 11), 11: (12,), 12: (13, 14), 14: (15,)}
NEAR_LAG = 1
OWN_LAG = 2


def pick(table, index):
    value = 0
    for k, v in enumerate(table):
        if v:
            value = value + jnp.where(index == k, v, 0)
    return value


def forwards(k):
    dp, dq = ORDER[k]
    out = []
    if dq == 0:
        if dp == 0:
            out.append((None, "p+", SLOT[3, 0]))
            out.append((None, "p-", SLOT[1, 0]))
        elif dp == 3:
            out.append((0, "p+", SLOT[2, 0]))
        elif dp == 1:
            out.append((1, "p-", SLOT[2, 0]))
        out.append((None, "q+", SLOT[dp, 3]))
        out.append((None, "q-", SLOT[dp, 1]))
    elif dq == 3:
        out.append((0, "q+", SLOT[dp, 2]))
    elif dq == 1:
        out.append((1, "q-", SLOT[dp, 2]))
    return out


SENDS = [(k, *copy) for k in range(STEPS) for copy in forwards(k)]


def in_halves(k):
    return 2 in ORDER[k] and ORDER[k] != (2, 1) and ORDER[k] != (2, 3)


def kernel(
    ab_sizes, cd_sizes, amp, integ, out,
    gath, right, acc, nearbuf, resbuf, far_s, far_r, near_s, near_r,
    amp_sem, int_sem, out_sem, ag_s, ag_r, sib_s, sib_r, far_ss, far_rs, near_ss, near_rs,
):
    cd_local, ab_local = right.shape
    unit = amp.shape[0]
    half = unit // 2
    blocks = ab_local // LANES
    index = lax.axis_index("ab")
    y = lax.axis_index("cd")
    c = index % 2
    x = (index // 2) % 4
    z = index // 8

    def at(z_, x_, c_):
        return ((z_ % 4) * 4 + x_ % 4) * 2 + c_

    def along(step, second):
        over_x = (1 - c) * (1 - second) + c * second
        return (at(z + step * (1 - over_x), x + step * over_x, c), y)

    target = {
        "p+": along(1, 0), "p-": along(3, 0), "q+": along(1, 1), "q-": along(3, 1),
        "core": (at(z, x, 1 - c), y), "y+": (index, (y + 1) % 4), "y-": (index, (y + 3) % 4),
    }

    tile_count = cd_local // TCD

    def int_copy(t):
        rows = pl.ds(pl.multiple_of(t * TCD, TCD), TCD)
        return pltpu.make_async_copy(integ.at[rows], right.at[rows], int_sem.at[t])

    amp_copy = pltpu.make_async_copy(amp, gath.at[0, 0], amp_sem)
    amp_copy.start()
    for t in range(tile_count):
        int_copy(t).start()

    barrier = pltpu.get_barrier_semaphore()
    for name in target:
        pl.semaphore_signal(barrier, inc=1, device_id=target[name], device_id_type=MESH)
    pl.semaphore_wait(barrier, len(target))

    def gather_copy(number, k, part, direction, slot):
        source = amp if k == 0 else gath.at[k, 0]
        dest = gath.at[slot, 0]
        if part is not None:
            source = source.at[pl.ds(part * half, half)]
            dest = dest.at[pl.ds(part * half, half)]
        return pltpu.make_async_remote_copy(
            src_ref=source, dst_ref=dest, send_sem=ag_s.at[number], recv_sem=ag_r.at[slot, part or 0],
            device_id=target[direction], device_id_type=MESH,
        )

    def sibling_copy(k):
        return pltpu.make_async_remote_copy(
            src_ref=amp if k == 0 else gath.at[k, 0], dst_ref=gath.at[k, 1],
            send_sem=sib_s.at[k], recv_sem=sib_r.at[k],
            device_id=target["core"], device_id_type=MESH,
        )

    def handle(k):
        if k:
            for part in (0, 1) if in_halves(k) else (None,):
                dest = gath.at[k, 0]
                if part is not None:
                    dest = dest.at[pl.ds(part * half, half)]
                pltpu.make_async_remote_copy(
                    src_ref=dest, dst_ref=dest, send_sem=ag_s.at[0], recv_sem=ag_r.at[k, part or 0],
                    device_id=target["p+"], device_id_type=MESH,
                ).wait_recv()
        for number, copy in enumerate(SENDS):
            if copy[0] == k:
                gather_copy(number, *copy).start()
        sibling_copy(k).start()

    handle(0)

    column = index * ab_local + lax.broadcasted_iota(jnp.int32, (1, ab_local), 1)

    def mask_tile(t, carry):
        place = y * cd_local + t * TCD
        low = 0
        high = 0
        end = 0
        for h in range(8):
            size = ab_sizes[h]
            high = high + jnp.where(end <= place, size, 0)
            end = end + cd_sizes[h]
            low = low + jnp.where(end <= place, size, 0)
        keep = jnp.where(jnp.logical_and(column >= low, column < high), 1.0, 0.0).astype(jnp.bfloat16)
        int_copy(t).wait()
        rows = pl.ds(pl.multiple_of(t * TCD, TCD), TCD)
        right[rows, :] = right[rows, :] * keep
        return carry

    lax.fori_loop(0, tile_count, mask_tile, 0)
    amp_copy.wait()

    def unit_place(s, net):
        dp = pick([d[0] for d in ORDER], s)
        dq = pick([d[1] for d in ORDER], s)
        core = (c + net) % 2
        dz = dq + core * (dp - dq)
        dx = dp + core * (dq - dp)
        return (z + dz - y + 8) % 4, ((x + dx) % 4) * 2 + core

    row_of = lax.broadcasted_iota(jnp.int32, (16, LANES), 0)

    def quantize(source, row, rows, dest):
        scales = jnp.zeros((16, LANES), jnp.float32)
        for j in range(blocks):
            value = source[pl.ds(row, rows), pl.ds(j * LANES, LANES)]
            most = jnp.max(jnp.abs(value), axis=0, keepdims=True)
            code = jnp.ceil(jnp.log2(jnp.maximum(most, 1e-30)) * FINE)
            factor = TOP / jnp.exp2(code * (1.0 / FINE))
            whole = jnp.floor(value * factor + 0.5).astype(jnp.int32).astype(jnp.int16)
            for i in range(rows // 16):
                dest[j * (rows // 16) + i] = whole[i * 16 : (i + 1) * 16]
            scales = jnp.where(row_of == j, code, scales)
        dest[blocks * (rows // 16)] = scales.astype(jnp.int32).astype(jnp.int16)

    def scales_of(source, rows):
        code = source[blocks * (rows // 16)].astype(jnp.int32).astype(jnp.float32)
        return jnp.exp2(code * (1.0 / FINE)) * (1.0 / TOP)

    def tiles_of(source, rows, j, scales):
        parts = [source[j * (rows // 16) + i].astype(jnp.int32).astype(jnp.float32) for i in range(rows // 16)]
        return jnp.concatenate(parts, axis=0) * scales[j : j + 1]

    def far_copy(slot, side):
        return pltpu.make_async_remote_copy(
            src_ref=far_s.at[side, slot], dst_ref=far_r.at[side, slot],
            send_sem=far_ss.at[side, slot], recv_sem=far_rs.at[side, slot],
            device_id=target["y-" if side else "y+"], device_id_type=MESH,
        )

    def near_copy(slot, side):
        return pltpu.make_async_remote_copy(
            src_ref=near_s.at[side, slot], dst_ref=near_r.at[side, slot],
            send_sem=near_ss.at[side, slot], recv_sem=near_rs.at[side, slot],
            device_id=target["y-" if side else "y+"], device_id_type=MESH,
        )

    def out_copy(slot):
        rows = pl.ds(pl.multiple_of(slot * unit, unit), unit)
        return pltpu.make_async_copy(resbuf.at[slot], out.at[rows], out_sem.at[slot])

    def after_product(s, net):
        role, slot = unit_place(s, net)

        @pl.when(role == 2)
        def _():
            for side in (0, 1):
                quantize(acc, net * unit + side * half, half, far_s.at[side, slot])
                far_copy(slot, side).start()

        for side, near in ((0, 1), (1, 3)):

            @pl.when(role == near)
            def _():
                nearbuf[side, slot] = acc[pl.ds(net * unit, unit), :]

        @pl.when(role == 0)
        def _():
            resbuf[slot] = acc[pl.ds(net * unit, unit), :]

    def near_stage(s, net):
        role, slot = unit_place(s, net)
        for side, near in ((0, 1), (1, 3)):

            @pl.when(role == near)
            def _():
                far_copy(slot, side).wait_recv()
                arrived = far_r.at[side, slot]
                scales = scales_of(arrived, half)
                for j in range(blocks):
                    cols = pl.ds(j * LANES, LANES)
                    rows = pl.ds(side * half, half)
                    nearbuf[side, slot, rows, cols] = nearbuf[side, slot, rows, cols] + tiles_of(arrived, half, j, scales)
                quantize(nearbuf.at[side, slot], 0, unit, near_s.at[side, slot])
                near_copy(slot, side).start()

    def own_stage(s, net):
        role, slot = unit_place(s, net)

        @pl.when(role == 0)
        def _():
            for side in (0, 1):
                near_copy(slot, side).wait_recv()
                arrived = near_r.at[side, slot]
                scales = scales_of(arrived, unit)
                for j in range(blocks):
                    cols = pl.ds(j * LANES, LANES)
                    resbuf[slot, :, cols] = resbuf[slot, :, cols] + tiles_of(arrived, unit, j, scales)
            out_copy(slot).start()

    def step(s, carry):
        for k, slots in HANDLE.items():

            @pl.when(s == k)
            def _():
                for slot in slots:
                    handle(slot)

        @pl.when(s < STEPS)
        def _():
            pltpu.make_async_remote_copy(
                src_ref=gath.at[s, 1], dst_ref=gath.at[s, 1], send_sem=sib_s.at[s], recv_sem=sib_r.at[s],
                device_id=target["core"], device_id_type=MESH,
            ).wait_recv()
            left = gath[s].reshape(2 * unit, cd_local)
            acc[...] = jnp.dot(left, right[...], preferred_element_type=jnp.float32)
            for net in (0, 1):
                after_product(s, net)

        @pl.when(jnp.logical_and(s >= NEAR_LAG, s < STEPS + NEAR_LAG))
        def _():
            for net in (0, 1):
                near_stage(s - NEAR_LAG, net)

        @pl.when(s >= OWN_LAG)
        def _():
            for net in (0, 1):
                own_stage(s - OWN_LAG, net)

        return carry

    lax.fori_loop(0, STEPS + OWN_LAG, step, 0)

    for number, copy in enumerate(SENDS):
        gather_copy(number, *copy).wait_send()
    for k in range(STEPS):
        sibling_copy(k).wait_send()

    def finish(slot, carry):
        for side in (0, 1):
            far_copy(slot, side).wait_send()
            near_copy(slot, side).wait_send()
        out_copy(slot).wait()
        return carry

    lax.fori_loop(0, 8, finish, 0)


def body(amplitudes, integrals, ab_sizes, cd_sizes, virt_energy, occ_energy):
    cd_local, ab_local = integrals.shape
    unit = amplitudes.shape[0]
    rows = occ_energy.shape[0]
    blocks = ab_local // LANES
    far = blocks * (unit // 32) + 1
    near = blocks * (unit // 16) + 1
    dma = pltpu.SemaphoreType.DMA
    residual = pl.pallas_call(
        kernel,
        out_shape=jax.ShapeDtypeStruct((rows, ab_local), jnp.float32),
        in_specs=[pl.BlockSpec(memory_space=pltpu.SMEM)] * 2 + [pl.BlockSpec(memory_space=pl.ANY)] * 2,
        out_specs=pl.BlockSpec(memory_space=pl.ANY),
        scratch_shapes=[
            pltpu.VMEM((STEPS, 2, unit, cd_local), jnp.bfloat16),
            pltpu.VMEM((cd_local, ab_local), jnp.bfloat16),
            pltpu.VMEM((2 * unit, ab_local), jnp.float32),
            pltpu.VMEM((2, 8, unit, ab_local), jnp.float32),
            pltpu.VMEM((8, unit, ab_local), jnp.float32),
            pltpu.VMEM((2, 8, far, 16, LANES), jnp.int16),
            pltpu.VMEM((2, 8, far, 16, LANES), jnp.int16),
            pltpu.VMEM((2, 8, near, 16, LANES), jnp.int16),
            pltpu.VMEM((2, 8, near, 16, LANES), jnp.int16),
            dma, dma((cd_local // TCD,)), dma((8,)), dma((20,)), dma((STEPS, 2)), dma((STEPS,)), dma((STEPS,)),
            dma((2, 8)), dma((2, 8)), dma((2, 8)), dma((2, 8)),
        ],
        compiler_params=pltpu.CompilerParams(
            collective_id=0, has_side_effects=True, vmem_limit_bytes=60 * 2**20
        ),
    )(ab_sizes, cd_sizes, amplitudes, integrals)
    update = residual / (virt_energy[None, :] - occ_energy[:, None])
    return (residual, update)


def solution(mesh):
    placed = (P("ab", "cd"), P("cd", "ab"), P(), P(), P("ab"), P("cd"))
    return jax.shard_map(
        body, mesh=mesh, in_specs=placed, out_specs=(P("cd", "ab"), P("cd", "ab")), check_vma=False
    )
```

time: 270 us -> 117 us (0.43); the launches traced: 267 us -> 117 us
  waiting for transfers between devices: 166 us -> 0 us
  Pallas kernels: 0 us -> 111 us
  matrix products: 75.5 us -> 0 us
  between operations: 14.1 us -> 0.68 us
  other arithmetic: 10.6 us -> 3.79 us
    pallas_call x0 -> x1, Pallas kernels: none -> 111 us  [body(): pl.pallas_call(kernel, out_shape=jax.ShapeDtypeStruct((rows, ab_local), j...]
    reduce_scatter x1 -> x0, waiting for transfers between devices: 95.5 us -> none  [body(): residual = lax.psum_scatter(total, 'cd', scatter_dimension=0, tiled=True)]
    dot_general x8 -> x0, matrix products: 75.5 us -> none  [body(): product = jnp.dot(left, right, preferred_element_type=jnp.float32)]
    all_gather x1 -> x0, waiting for transfers between devices: 69.5 us -> none  [body(): rows = lax.all_gather(amplitudes, 'ab', axis=0, tiled=True)]
    eq x1 -> x0, other arithmetic: 5.02 us -> none  [body(): column_irrep[None, :] == irrep]
  transfers between devices with their start and end apart: 2 -> 0, of which waited for: 2 -> 0; matrix products, arithmetic and copies ran while one was open for 3% -> 0% of each run, Pallas kernels for 0% -> 0%
where the time goes in v1:
time: 117 us
  Pallas kernels  111 us (95%)
  other arithmetic  3.79 us (3%)
  local copies, waits for them, and re-layouts  1.5 us (1%)
    pallas_call x1, Pallas kernels, body(): pl.pallas_call(kernel, out_shape=jax.ShapeDtypeStruct((rows, ab_local), j...  111 us
    div x1, other arithmetic, body(): update = residual / (virt_energy[None, :] - occ_energy[:, None])  3.79 us

profile of v1, /device:TPU:18, one launch (start us, length us, event | category | flops | bytes accessed | tf_op | source)
XLA Modules:
  0.0 117.3 jit_solution(5450449445440290155)
XLA Ops:
  0.6 0.0 copy-start.2
  0.6 0.0 copy-start.1
  0.7 111.4 %shard_map.77 = f32[512,1280]{1,0:T(8,128)} custom-call(s32[8]{0:T(128)} %ab_sizes.1, s32[8]{0:T(128)} %cd_sizes.1, bf16[64,4096]{1,0:T(8,128)(2,1)} %amp.1, bf16[4096,1280]{1,0:T(8,128)(2,1)} %integ.1), custom_call_target="tpu_custom_call" | custom-call | tf_op jit(solution)/shard_map/pallas_call | solution.py:315
  112.0 0.0 copy-done.2
  112.0 0.0 copy-done.1
  112.0 0.0 copy-start
  112.0 3.8 %subtract_divide_fusion = f32[512,1280]{1,0:T(8,128)} fusion(f32[512,1280]{1,0:T(8,128)} %shard_map.77, f32[512]{0:T(512)S(1)} %copy-done.2, f32[1280]{0:T(1024)S(1)} %copy-done.1), kind=kLoop, calls=%fused_computation | loop fusion | flops 1310720 | bytes 5250048 | tf_op jit(solution)/shard_map/div | solution.py:337
  115.8 0.0 copy-done
  115.8 1.5 %copy.9 = f32[512,1280]{1,0:T(8,128)} copy(f32[512,1280]{1,0:T(8,128)S(1)} %copy-done) | data formatting | bytes 5242880
Async XLA Ops:
  0.6 111.4 %copy-start.2 = (f32[512]{0:T(512)S(1)}, f32[512]{0:T(512)}, u32[]{:S(2)}) copy-start(f32[512]{0:T(512)} %param.11) | copy-start | bytes 6148
  0.6 111.4 %copy-start.1 = (f32[1280]{0:T(1024)S(1)}, f32[1280]{0:T(1024)}, u32[]{:S(2)}) copy-start(f32[1280]{0:T(1024)} %param.10) | copy-start | bytes 15364
  112.0 3.8 %copy-start = (f32[512,1280]{1,0:T(8,128)S(1)}, f32[512,1280]{1,0:T(8,128)}, u32[]{:S(2)}) copy-start(f32[512,1280]{1,0:T(8,128)} %shard_map.77) | copy-start | bytes 7864324

commit v2 on v1

--- a/solution.py
+++ b/solution.py
@@ -13,50 +13,37 @@
 TOP = 32000.0
 FINE = 64.0
 
-ORDER = (
-    (0, 0), (1, 0), (3, 0), (0, 1), (0, 3), (2, 0), (0, 2), (1, 1),
-    (1, 3), (1, 2), (3, 1), (3, 3), (3, 2), (2, 1), (2, 3), (2, 2),
+GROUPS = ((4, 12), (8,)) + tuple((4 * d + 1, 4 * d + 3) for d in range(4)) + tuple((4 * d + 2,) for d in range(4))
+PASSED = ((0,), (4, 12), (8,))
+STEPS = 16
+
+ACTIONS = (
+    (
+        5, 20, 4096, 3, 3104, 1, 129, 13, 28, 12, 44, 7328, 33, 19, 5000, 97, 2, 776,
+        21, 36, 52, 130, 161, 27, 60, 225, 5568, 137, 153, 11, 2232, 34, 162, 226, 1832, 193,
+        9, 25, 98, 65, 43, 7440, 169, 1784, 138, 35, 7112, 68, 76, 17, 10, 26, 185, 194,
+        51, 154, 170, 57, 49, 2448, 59, 201, 41, 233, 217, 5720, 67, 249, 58, 66, 18, 145,
+        3536, 75, 7800, 186, 50, 234, 202, 73, 250, 218, 42, 89, 177, 3664, 209, 146, 121, 105,
+        241, 74, 210, 90, 178, 81, 113, 122, 242, 82, 106, 114,
+    ),
+    (
+        5, 20, 4096, 3, 12, 3104, 1, 13, 28, 7328, 129, 33, 19, 52, 97, 5000, 11, 2056,
+        161, 225, 2, 34, 130, 98, 65, 27, 60, 6056, 9, 137, 153, 51, 4648, 21, 36, 44,
+        1816, 59, 5824, 138, 145, 66, 162, 154, 226, 3944, 25, 185, 169, 177, 193, 35, 68, 7112,
+        2888, 41, 146, 10, 186, 178, 57, 43, 76, 7952, 105, 121, 1768, 67, 73, 89, 6736, 75,
+        201, 217, 3824, 17, 249, 170, 26, 194, 42, 58, 106, 233, 122, 49, 81, 209, 74, 202,
+        218, 18, 90, 113, 241, 82, 210, 250, 234, 242, 50, 114,
+    ),
 )
-SLOT = {d: k for k, d in enumerate(ORDER)}
-STEPS = len(ORDER)
-HANDLE = {1: (1, 2), 2: (3, 4), 4: (5, 6), 6: (7, 8), 8: (9,), 9: (10, 11), 11: (12,), 12: (13, 14), 14: (15,)}
-NEAR_LAG = 1
-OWN_LAG = 2
 
 
 def pick(table, index):
-    value = 0
-    for k, v in enumerate(table):
-        if v:
-            value = value + jnp.where(index == k, v, 0)
-    return value
-
-
-def forwards(k):
-    dp, dq = ORDER[k]
-    out = []
-    if dq == 0:
-        if dp == 0:
-            out.append((None, "p+", SLOT[3, 0]))
-            out.append((None, "p-", SLOT[1, 0]))
-        elif dp == 3:
-            out.append((0, "p+", SLOT[2, 0]))
-        elif dp == 1:
-            out.append((1, "p-", SLOT[2, 0]))
-        out.append((None, "q+", SLOT[dp, 3]))
-        out.append((None, "q-", SLOT[dp, 1]))
-    elif dq == 3:
-        out.append((0, "q+", SLOT[dp, 2]))
-    elif dq == 1:
-        out.append((1, "q-", SLOT[dp, 2]))
-    return out
-
-
-SENDS = [(k, *copy) for k in range(STEPS) for copy in forwards(k)]
-
-
-def in_halves(k):
-    return 2 in ORDER[k] and ORDER[k] != (2, 1) and ORDER[k] != (2, 3)
+    words = [low + 8192 * high for low, high in zip(table[::2], table[1::2] + (0,))]
+    at = index // 2
+    word = words[0]
+    for w in range(1, len(words)):
+        word = jnp.where(at == w, words[w], word)
+    return jnp.where(index % 2 == 0, word, word // 8192) % 8192
 
 
 def kernel(
@@ -77,12 +64,11 @@
     def at(z_, x_, c_):
         return ((z_ % 4) * 4 + x_ % 4) * 2 + c_
 
-    def along(step, second):
-        over_x = (1 - c) * (1 - second) + c * second
-        return (at(z + step * (1 - over_x), x + step * over_x, c), y)
+    def along(step):
+        return (at(z + step * c, x + step * (1 - c), c), y)
 
     target = {
-        "p+": along(1, 0), "p-": along(3, 0), "q+": along(1, 1), "q-": along(3, 1),
+        "+": along(1), "-": along(3),
         "core": (at(z, x, 1 - c), y), "y+": (index, (y + 1) % 4), "y-": (index, (y + 3) % 4),
     }
 
@@ -102,40 +88,54 @@
         pl.semaphore_signal(barrier, inc=1, device_id=target[name], device_id_type=MESH)
     pl.semaphore_wait(barrier, len(target))
 
-    def gather_copy(number, k, part, direction, slot):
-        source = amp if k == 0 else gath.at[k, 0]
-        dest = gath.at[slot, 0]
+    def gather_copy(g, side):
+        part = None
+        if g == 0:
+            source, slot, gather = amp, (12, 4)[side], 0
+        elif g == 1:
+            source, slot, gather, part = gath.at[(12, 4)[side], 0], 8, 0, side
+        elif g < 6:
+            d = 4 * (g - 2)
+            source, slot, gather = gath.at[d, 1], d + (3, 1)[side], 1
+        else:
+            d = 4 * (g - 6)
+            source, slot, gather, part = gath.at[d + (3, 1)[side], 1], d + 2, 1, side
+        dest = gath.at[slot, gather]
         if part is not None:
             source = source.at[pl.ds(part * half, half)]
             dest = dest.at[pl.ds(part * half, half)]
         return pltpu.make_async_remote_copy(
-            src_ref=source, dst_ref=dest, send_sem=ag_s.at[number], recv_sem=ag_r.at[slot, part or 0],
-            device_id=target[direction], device_id_type=MESH,
+            src_ref=source, dst_ref=dest, send_sem=ag_s.at[g, side], recv_sem=ag_r.at[slot, part or 0],
+            device_id=target["-" if side else "+"], device_id_type=MESH,
         )
 
     def sibling_copy(k):
+        gather = 0 if k % 4 == 0 else 1
         return pltpu.make_async_remote_copy(
-            src_ref=amp if k == 0 else gath.at[k, 0], dst_ref=gath.at[k, 1],
+            src_ref=amp if k == 0 else gath.at[k, gather], dst_ref=gath.at[k, 1 - gather],
             send_sem=sib_s.at[k], recv_sem=sib_r.at[k],
             device_id=target["core"], device_id_type=MESH,
         )
 
-    def handle(k):
-        if k:
-            for part in (0, 1) if in_halves(k) else (None,):
-                dest = gath.at[k, 0]
-                if part is not None:
-                    dest = dest.at[pl.ds(part * half, half)]
-                pltpu.make_async_remote_copy(
-                    src_ref=dest, dst_ref=dest, send_sem=ag_s.at[0], recv_sem=ag_r.at[k, part or 0],
-                    device_id=target["p+"], device_id_type=MESH,
-                ).wait_recv()
-        for number, copy in enumerate(SENDS):
-            if copy[0] == k:
-                gather_copy(number, *copy).start()
-        sibling_copy(k).start()
-
-    handle(0)
+    def issue(g):
+        for side in (0, 1):
+            gather_copy(g, side).start()
+
+    def handle(g):
+        for side in (0, 1):
+            gather_copy(g, side).wait_recv()
+        for k in GROUPS[g]:
+            sibling_copy(k).start()
+
+    def passed(g):
+        for k in PASSED[g]:
+            pltpu.make_async_remote_copy(
+                src_ref=gath.at[k, 1], dst_ref=gath.at[k, 1], send_sem=sib_s.at[k], recv_sem=sib_r.at[k],
+                device_id=target["core"], device_id_type=MESH,
+            ).wait_recv()
+
+    issue(0)
+    sibling_copy(0).start()
 
     column = index * ab_local + lax.broadcasted_iota(jnp.int32, (1, ab_local), 1)
 
@@ -158,9 +158,10 @@
     lax.fori_loop(0, tile_count, mask_tile, 0)
     amp_copy.wait()
 
-    def unit_place(s, net):
-        dp = pick([d[0] for d in ORDER], s)
-        dq = pick([d[1] for d in ORDER], s)
+    def unit_place(u):
+        net = u // 16
+        dp = (u % 16) // 4
+        dq = u % 4
         core = (c + net) % 2
         dz = dq + core * (dp - dq)
         dx = dp + core * (dq - dp)
@@ -207,8 +208,8 @@
         rows = pl.ds(pl.multiple_of(slot * unit, unit), unit)
         return pltpu.make_async_copy(resbuf.at[slot], out.at[rows], out_sem.at[slot])
 
-    def after_product(s, net):
-        role, slot = unit_place(s, net)
+    def after_product(u, net):
+        role, slot = unit_place(u)
 
         @pl.when(role == 2)
         def _():
@@ -226,8 +227,8 @@
         def _():
             resbuf[slot] = acc[pl.ds(net * unit, unit), :]
 
-    def near_stage(s, net):
-        role, slot = unit_place(s, net)
+    def near_stage(u):
+        role, slot = unit_place(u)
         for side, near in ((0, 1), (1, 3)):
 
             @pl.when(role == near)
@@ -242,8 +243,8 @@
                 quantize(nearbuf.at[side, slot], 0, unit, near_s.at[side, slot])
                 near_copy(slot, side).start()
 
-    def own_stage(s, net):
-        role, slot = unit_place(s, net)
+    def own_stage(u):
+        role, slot = unit_place(u)
 
         @pl.when(role == 0)
         def _():
@@ -256,41 +257,55 @@
                     resbuf[slot, :, cols] = resbuf[slot, :, cols] + tiles_of(arrived, unit, j, scales)
             out_copy(slot).start()
 
-    def step(s, carry):
-        for k, slots in HANDLE.items():
-
-            @pl.when(s == k)
+    def product(first, second):
+        for u in (first, second):
+
+            @pl.when(jnp.logical_and(u < 16, u % 4 != 0))
             def _():
-                for slot in slots:
-                    handle(slot)
-
-        @pl.when(s < STEPS)
-        def _():
-            pltpu.make_async_remote_copy(
-                src_ref=gath.at[s, 1], dst_ref=gath.at[s, 1], send_sem=sib_s.at[s], recv_sem=sib_r.at[s],
-                device_id=target["core"], device_id_type=MESH,
-            ).wait_recv()
-            left = gath[s].reshape(2 * unit, cd_local)
-            acc[...] = jnp.dot(left, right[...], preferred_element_type=jnp.float32)
-            for net in (0, 1):
-                after_product(s, net)
-
-        @pl.when(jnp.logical_and(s >= NEAR_LAG, s < STEPS + NEAR_LAG))
-        def _():
-            for net in (0, 1):
-                near_stage(s - NEAR_LAG, net)
-
-        @pl.when(s >= OWN_LAG)
-        def _():
-            for net in (0, 1):
-                own_stage(s - OWN_LAG, net)
+                pltpu.make_async_remote_copy(
+                    src_ref=gath.at[u, 0], dst_ref=gath.at[u, 0], send_sem=sib_s.at[u], recv_sem=sib_r.at[u],
+                    device_id=target["core"], device_id_type=MESH,
+                ).wait_recv()
+
+        left = jnp.concatenate([gath[u % 16, u // 16] for u in (first, second)], axis=0)
+        acc[...] = jnp.dot(left, right[...], preferred_element_type=jnp.float32)
+        after_product(first, 0)
+        after_product(second, 1)
+
+    def act(a, carry):
+        code = jnp.where(c == 0, pick(ACTIONS[0], a), pick(ACTIONS[1], a))
+        kind = code % 8
+        arg = (code // 8) % 32
+
+        @pl.when(kind == 0)
+        def _():
+            product(arg, code // 256)
+
+        @pl.when(kind == 1)
+        def _():
+            near_stage(arg)
+
+        @pl.when(kind == 2)
+        def _():
+            own_stage(arg)
+
+        for this, count, do in ((3, len(GROUPS), handle), (4, len(GROUPS), issue), (5, len(PASSED), passed)):
+
+            @pl.when(kind == this)
+            def _():
+                for g in range(count):
+
+                    @pl.when(arg == g)
+                    def _():
+                        do(g)
 
         return carry
 
-    lax.fori_loop(0, STEPS + OWN_LAG, step, 0)
-
-    for number, copy in enumerate(SENDS):
-        gather_copy(number, *copy).wait_send()
+    lax.fori_loop(0, len(ACTIONS[0]), act, 0)
+
+    for g in range(len(GROUPS)):
+        for side in (0, 1):
+            gather_copy(g, side).wait_send()
     for k in range(STEPS):
         sibling_copy(k).wait_send()
 
@@ -327,7 +342,7 @@
             pltpu.VMEM((2, 8, far, 16, LANES), jnp.int16),
             pltpu.VMEM((2, 8, near, 16, LANES), jnp.int16),
             pltpu.VMEM((2, 8, near, 16, LANES), jnp.int16),
-            dma, dma((cd_local // TCD,)), dma((8,)), dma((20,)), dma((STEPS, 2)), dma((STEPS,)), dma((STEPS,)),
+            dma, dma((cd_local // TCD,)), dma((8,)), dma((10, 2)), dma((STEPS, 2)), dma((STEPS,)), dma((STEPS,)),
             dma((2, 8)), dma((2, 8)), dma((2, 8)), dma((2, 8)),
         ],
         compiler_params=pltpu.CompilerParams(

time: 117 us -> 84.4 us (0.72)
  Pallas kernels: 111 us -> 77.7 us
    pallas_call x1, Pallas kernels: 111 us -> 77.7 us  [body(): pl.pallas_call(kernel, out_shape=jax.ShapeDtypeStruct((rows, ab_local), j...]
where the time goes in v2:
time: 84.4 us; the launch traced here: 83.7 us
  Pallas kernels  77.7 us (92%)
  other arithmetic  3.79 us (4%)
  local copies, waits for them, and re-layouts  1.5 us (2%)
    pallas_call x1, Pallas kernels, body(): pl.pallas_call(kernel, out_shape=jax.ShapeDtypeStruct((rows, ab_local), j...  77.7 us
    div x1, other arithmetic, body(): update = residual / (virt_energy[None, :] - occ_energy[:, None])  3.79 us

profile of v2, /device:TPU:18, one launch (start us, length us, event | category | flops | bytes accessed | tf_op | source)
XLA Modules:
  0.0 83.7 jit_solution(14506306516858685904)
XLA Ops:
  0.6 0.0 copy-start.2
  0.6 0.0 copy-start.1
  0.7 77.7 %shard_map.77 = f32[512,1280]{1,0:T(8,128)} custom-call(s32[8]{0:T(128)} %ab_sizes.1, s32[8]{0:T(128)} %cd_sizes.1, bf16[64,4096]{1,0:T(8,128)(2,1)} %amp.1, bf16[4096,1280]{1,0:T(8,128)(2,1)} %integ.1), custom_call_target="tpu_custom_call" | custom-call | tf_op jit(solution)/shard_map/pallas_call | solution.py:330
  78.3 0.0 copy-done.2
  78.3 0.0 copy-done.1
  78.4 0.0 copy-start
  78.4 3.8 %subtract_divide_fusion = f32[512,1280]{1,0:T(8,128)} fusion(f32[512,1280]{1,0:T(8,128)} %shard_map.77, f32[512]{0:T(512)S(1)} %copy-done.2, f32[1280]{0:T(1024)S(1)} %copy-done.1), kind=kLoop, calls=%fused_computation | loop fusion | flops 1310720 | bytes 5250048 | tf_op jit(solution)/shard_map/div | solution.py:352
  82.2 0.0 copy-done
  82.2 1.5 %copy.9 = f32[512,1280]{1,0:T(8,128)} copy(f32[512,1280]{1,0:T(8,128)S(1)} %copy-done) | data formatting | bytes 5242880
Async XLA Ops:
  0.6 77.7 %copy-start.2 = (f32[512]{0:T(512)S(1)}, f32[512]{0:T(512)}, u32[]{:S(2)}) copy-start(f32[512]{0:T(512)} %param.11) | copy-start | bytes 6148
  0.6 77.7 %copy-start.1 = (f32[1280]{0:T(1024)S(1)}, f32[1280]{0:T(1024)}, u32[]{:S(2)}) copy-start(f32[1280]{0:T(1024)} %param.10) | copy-start | bytes 15364
  78.4 3.8 %copy-start = (f32[512,1280]{1,0:T(8,128)S(1)}, f32[512,1280]{1,0:T(8,128)}, u32[]{:S(2)}) copy-start(f32[512,1280]{1,0:T(8,128)} %shard_map.77) | copy-start | bytes 7864324

commit v3 on v2

--- a/solution.py
+++ b/solution.py
@@ -19,20 +19,20 @@
 
 ACTIONS = (
     (
-        5, 20, 4096, 3, 3104, 1, 129, 13, 28, 12, 44, 7328, 33, 19, 5000, 97, 2, 776,
-        21, 36, 52, 130, 161, 27, 60, 225, 5568, 137, 153, 11, 2232, 34, 162, 226, 1832, 193,
-        9, 25, 98, 65, 43, 7440, 169, 1784, 138, 35, 7112, 68, 76, 17, 10, 26, 185, 194,
-        51, 154, 170, 57, 49, 2448, 59, 201, 41, 233, 217, 5720, 67, 249, 58, 66, 18, 145,
-        3536, 75, 7800, 186, 50, 234, 202, 73, 250, 218, 42, 89, 177, 3664, 209, 146, 121, 105,
-        241, 74, 210, 90, 178, 81, 113, 122, 242, 82, 106, 114,
+        5, 4096, 3, 12, 3104, 1, 129, 13, 28, 44, 7328, 33, 11, 2, 320, 130, 21, 36,
+        20, 97, 27, 161, 6168, 225, 6056, 65, 34, 193, 43, 7528, 9, 4088, 98, 162, 25, 3600,
+        35, 68, 60, 76, 169, 185, 7112, 10, 194, 66, 226, 233, 26, 249, 19, 52, 4392, 17,
+        121, 1944, 113, 105, 67, 170, 2512, 59, 137, 41, 201, 217, 18, 5720, 75, 57, 7728, 51,
+        73, 202, 4688, 153, 186, 234, 114, 250, 89, 177, 138, 122, 106, 218, 209, 154, 241, 42,
+        145, 210, 58, 49, 74, 146, 81, 90, 178, 50, 242, 82,
     ),
     (
-        5, 20, 4096, 3, 12, 3104, 1, 13, 28, 7328, 129, 33, 19, 52, 97, 5000, 11, 2056,
-        161, 225, 2, 34, 130, 98, 65, 27, 60, 6056, 9, 137, 153, 51, 4648, 21, 36, 44,
-        1816, 59, 5824, 138, 145, 66, 162, 154, 226, 3944, 25, 185, 169, 177, 193, 35, 68, 7112,
-        2888, 41, 146, 10, 186, 178, 57, 43, 76, 7952, 105, 121, 1768, 67, 73, 89, 6736, 75,
-        201, 217, 3824, 17, 249, 170, 26, 194, 42, 58, 106, 233, 122, 49, 81, 209, 74, 202,
-        218, 18, 90, 113, 241, 82, 210, 250, 234, 242, 50, 114,
+        5, 20, 4096, 3, 12, 3104, 1, 13, 44, 7328, 129, 33, 19, 97, 52, 5000, 21, 11,
+        2240, 161, 225, 2, 34, 98, 43, 76, 28, 36, 8168, 193, 153, 65, 137, 51, 1832, 75,
+        7824, 3944, 130, 66, 162, 154, 226, 233, 145, 249, 138, 27, 60, 6056, 241, 2888, 41, 194,
+        57, 105, 146, 121, 35, 68, 6408, 169, 984, 59, 185, 5712, 67, 73, 89, 250, 242, 1744,
+        201, 217, 106, 42, 9, 58, 624, 25, 170, 74, 234, 10, 186, 81, 122, 177, 209, 90,
+        49, 113, 26, 17, 18, 114, 202, 218, 210, 50, 82, 178,
     ),
 )
 
@@ -317,6 +317,15 @@
         return carry
 
     lax.fori_loop(0, 8, finish, 0)
+
+
+def divide(sums, virt, occ, residual, update):
+    rows = jnp.concatenate([jnp.transpose(jnp.broadcast_to(occ[pl.ds(pl.multiple_of(pl.program_id(0) * 256 + i * LANES, LANES), LANES)].reshape(1, LANES), (LANES, LANES))) for i in range(256 // LANES)], axis=0)
+    for j in range(sums.shape[1] // LANES):
+        cols = pl.ds(j * LANES, LANES)
+        value = sums[:, cols]
+        residual[:, cols] = value
+        update[:, cols] = value / (virt[cols].reshape(1, LANES) - rows)
 
 
 def body(amplitudes, integrals, ab_sizes, cd_sizes, virt_energy, occ_energy):
@@ -349,8 +358,15 @@
             collective_id=0, has_side_effects=True, vmem_limit_bytes=60 * 2**20
         ),
     )(ab_sizes, cd_sizes, amplitudes, integrals)
-    update = residual / (virt_energy[None, :] - occ_energy[:, None])
-    return (residual, update)
+    tile = pl.BlockSpec((256, ab_local), lambda i: (i, 0))
+    return pl.pallas_call(
+        divide,
+        grid=(rows // 256,),
+        out_shape=(jax.ShapeDtypeStruct((rows, ab_local), jnp.float32),) * 2,
+        in_specs=[tile, pl.BlockSpec((ab_local,), lambda i: (0,)), pl.BlockSpec((rows,), lambda i: (0,))],
+        out_specs=(tile, tile),
+        compiler_params=pltpu.CompilerParams(vmem_limit_bytes=60 * 2**20),
+    )(residual, virt_energy, occ_energy)
 
 
 def solution(mesh):

time: 84.4 us -> 82.4 us (0.976)
  other arithmetic: 3.79 us -> 0 us
  Pallas kernels: 77.7 us -> 81.3 us
  local copies, waits for them, and re-layouts: 1.5 us -> 0 us
    pallas_call x0 -> x1, Pallas kernels: none -> 3.89 us  [body(): pl.pallas_call(divide, grid=(rows // 256,), out_shape=(jax.ShapeDtypeStru...]
    div x1 -> x0, other arithmetic: 3.79 us -> none  [body(): update = residual / (virt_energy[None, :] - occ_energy[:, None])]
    unnamed x7 -> x0, local copies, waits for them, and re-layouts: 1.5 us -> none
where the time goes in v3:
time: 82.4 us; the launch traced here: 81.9 us
  Pallas kernels  81.3 us (99%)
    pallas_call x1, Pallas kernels, body(): pl.pallas_call(kernel, out_shape=jax.ShapeDtypeStruct((rows, ab_local), j...  77.4 us
    pallas_call x1, Pallas kernels, body(): pl.pallas_call(divide, grid=(rows // 256,), out_shape=(jax.ShapeDtypeStru...  3.89 us

profile of v3, /device:TPU:18, one launch (start us, length us, event | category | flops | bytes accessed | tf_op | source)
XLA Modules:
  0.0 81.9 jit_solution(17192956315056803296)
XLA Ops:
  0.6 77.4 %shard_map.77.sums = f32[512,1280]{1,0:T(8,128)} custom-call(s32[8]{0:T(128)} %ab_sizes.1, s32[8]{0:T(128)} %cd_sizes.1, bf16[64,4096]{1,0:T(8,128)(2,1)} %amp.1, bf16[4096,1280]{1,0:T(8,128)(2,1)} %integ.1), custom_call_target="tpu_custom_call" | custom-call | tf_op jit(solution)/shard_map/pallas_call | solution.py:339
  78.0 3.9 %shard_map.78 = (f32[512,1280]{1,0:T(8,128)}, f32[512,1280]{1,0:T(8,128)}) custom-call(f32[512,1280]{1,0:T(8,128)} %shard_map.77.sums, f32[1280]{0:T(1024)} %virt.1, f32[512]{0:T(512)} %occ.1), custom_call_target="tpu_custom_call" | custom-call | tf_op jit(solution)/shard_map/pallas_call | solution.py:362

commit v4 on v3

--- a/solution.py
+++ b/solution.py
@@ -13,37 +13,58 @@
 TOP = 32000.0
 FINE = 64.0
 
-GROUPS = ((4, 12), (8,)) + tuple((4 * d + 1, 4 * d + 3) for d in range(4)) + tuple((4 * d + 2,) for d in range(4))
-PASSED = ((0,), (4, 12), (8,))
+COPIES = (
+    ("first", 0, 0), ("first", 0, 1), ("across", 0, None), ("second", 0, None), ("second", 1, 0), ("second", 1, 1),
+    ("second", 2, None), ("second", 3, 0), ("second", 3, 1), ("last", 0, None), ("last", 1, None), ("last", 2, None),
+    ("last", 3, None),
+)
+ARRIVALS = (
+    ((0,), (4, 12), 0), ((1,), (4, 12), 1), ((2,), (8,), None), ((3,), (1, 3), None), ((4, 5), (5, 7), None),
+    ((6,), (9, 11), None), ((7, 8), (13, 15), None), ((9,), (2,), None), ((10,), (6,), None), ((11,), (10,), None),
+    ((12,), (14,), None),
+)
+PASSED = (((0,), None), ((4, 12), 0), ((4, 12), 1), ((8,), None))
 STEPS = 16
 
+UNITS = (
+    (
+        0, 16, 4, 12, 20, 28, 8, 1, 3, 24, 21, 23, 13, 29, 31, 15, 2, 14, 25, 27, 5, 17, 19, 7, 26, 9,
+        11, 22, 6, 30, 10, 18,
+    ),
+    (
+        0, 16, 4, 12, 20, 28, 17, 19, 24, 8, 29, 31, 5, 7, 18, 30, 13, 15, 21, 23, 9, 11, 1, 25, 27, 3,
+        10, 22, 26, 6, 14, 2,
+    ),
+)
 ACTIONS = (
     (
-        5, 4096, 3, 12, 3104, 1, 129, 13, 28, 44, 7328, 33, 11, 2, 320, 130, 21, 36,
-        20, 97, 27, 161, 6168, 225, 6056, 65, 34, 193, 43, 7528, 9, 4088, 98, 162, 25, 3600,
-        35, 68, 60, 76, 169, 185, 7112, 10, 194, 66, 226, 233, 26, 249, 19, 52, 4392, 17,
-        121, 1944, 113, 105, 67, 170, 2512, 59, 137, 41, 201, 217, 18, 5720, 75, 57, 7728, 51,
-        73, 202, 4688, 153, 186, 234, 114, 250, 89, 177, 138, 122, 106, 218, 209, 154, 241, 42,
-        145, 210, 58, 49, 74, 146, 81, 90, 178, 50, 242, 82,
+        5, 0, 3, 11, 20, 8, 1, 9, 13, 21, 36, 44, 60, 68, 16, 17, 19, 2, 24, 10, 29, 52, 28, 25, 35, 33,
+        32, 41, 40, 49, 18, 73, 51, 48, 57, 56, 26, 34, 65, 64, 43, 92, 84, 100, 81, 89, 72, 58, 74, 50, 42, 105,
+        66, 113, 27, 76, 80, 129, 121, 88, 137, 97, 75, 82, 96, 67, 169, 161, 145, 153, 130, 104, 83, 185, 112, 59, 201, 146,
+        120, 177, 90, 106, 138, 114, 209, 217, 170, 122, 98, 154, 193, 178, 233, 162, 249, 194, 186, 225, 202, 250, 241, 210, 218, 226,
+        234, 242,
     ),
     (
-        5, 20, 4096, 3, 12, 3104, 1, 13, 44, 7328, 129, 33, 19, 97, 52, 5000, 21, 11,
-        2240, 161, 225, 2, 34, 98, 43, 76, 28, 36, 8168, 193, 153, 65, 137, 51, 1832, 75,
-        7824, 3944, 130, 66, 162, 154, 226, 233, 145, 249, 138, 27, 60, 6056, 241, 2888, 41, 194,
-        57, 105, 146, 121, 35, 68, 6408, 169, 984, 59, 185, 5712, 67, 73, 89, 250, 242, 1744,
-        201, 217, 106, 42, 9, 58, 624, 25, 170, 74, 234, 10, 186, 81, 122, 177, 209, 90,
-        49, 113, 26, 17, 18, 114, 202, 218, 210, 50, 82, 178,
+        5, 28, 0, 3, 11, 20, 8, 1, 13, 21, 60, 68, 16, 9, 17, 27, 25, 76, 24, 29, 19, 32, 33, 41, 2, 18,
+        26, 51, 100, 36, 44, 52, 40, 65, 57, 73, 49, 59, 48, 83, 56, 64, 10, 74, 34, 58, 42, 81, 113, 89, 50, 35,
+        84, 72, 121, 80, 97, 66, 105, 129, 114, 137, 43, 92, 88, 145, 96, 67, 153, 104, 75, 161, 169, 90, 122, 112, 185, 193,
+        130, 98, 177, 106, 120, 201, 146, 162, 82, 178, 154, 209, 138, 217, 225, 170, 233, 241, 202, 249, 250, 242, 186, 194, 226, 234,
+        210, 218,
     ),
 )
-
-
-def pick(table, index):
-    words = [low + 8192 * high for low, high in zip(table[::2], table[1::2] + (0,))]
-    at = index // 2
+PLACE = tuple({u: i for i, u in enumerate(units)} for units in UNITS)
+
+
+def pick(table, bits, index):
+    words = []
+    for w in range(0, len(table), 4):
+        word = sum(v << (bits * i) for i, v in enumerate(table[w : w + 4]))
+        words.append(word - 2**32 if word >= 2**31 else word)
+    at = index >> 2
     word = words[0]
     for w in range(1, len(words)):
         word = jnp.where(at == w, words[w], word)
-    return jnp.where(index % 2 == 0, word, word // 8192) % 8192
+    return (word >> ((index & 3) * bits)) & (2**bits - 1)
 
 
 def kernel(
@@ -78,7 +99,7 @@
         rows = pl.ds(pl.multiple_of(t * TCD, TCD), TCD)
         return pltpu.make_async_copy(integ.at[rows], right.at[rows], int_sem.at[t])
 
-    amp_copy = pltpu.make_async_copy(amp, gath.at[0, 0], amp_sem)
+    amp_copy = pltpu.make_async_copy(amp, gath.at[jnp.where(c == 0, PLACE[0][0], PLACE[1][0])], amp_sem)
     amp_copy.start()
     for t in range(tile_count):
         int_copy(t).start()
@@ -88,32 +109,34 @@
         pl.semaphore_signal(barrier, inc=1, device_id=target[name], device_id_type=MESH)
     pl.semaphore_wait(barrier, len(target))
 
+    def place(k, gather, core=0):
+        unit_at = k + 16 * (gather if core == 0 else 1 - gather)
+        return gath.at[jnp.where(c == core, PLACE[0][unit_at], PLACE[1][unit_at])]
+
+    def rows_of(ref, part):
+        return ref if part is None else ref.at[pl.ds(part * half, half)]
+
     def gather_copy(g, side):
-        part = None
-        if g == 0:
+        what, d, part = COPIES[g]
+        if what == "first":
             source, slot, gather = amp, (12, 4)[side], 0
-        elif g == 1:
-            source, slot, gather, part = gath.at[(12, 4)[side], 0], 8, 0, side
-        elif g < 6:
-            d = 4 * (g - 2)
-            source, slot, gather = gath.at[d, 1], d + (3, 1)[side], 1
+        elif what == "across":
+            source, slot, gather, part = place((12, 4)[side], 0), 8, 0, side
+        elif what == "second":
+            source, slot, gather = place(4 * d, 1), 4 * d + (3, 1)[side], 1
         else:
-            d = 4 * (g - 6)
-            source, slot, gather, part = gath.at[d + (3, 1)[side], 1], d + 2, 1, side
-        dest = gath.at[slot, gather]
-        if part is not None:
-            source = source.at[pl.ds(part * half, half)]
-            dest = dest.at[pl.ds(part * half, half)]
+            source, slot, gather, part = place(4 * d + (3, 1)[side], 1), 4 * d + 2, 1, side
         return pltpu.make_async_remote_copy(
-            src_ref=source, dst_ref=dest, send_sem=ag_s.at[g, side], recv_sem=ag_r.at[slot, part or 0],
+            src_ref=rows_of(source, part), dst_ref=rows_of(place(slot, gather), part),
+            send_sem=ag_s.at[g, side], recv_sem=ag_r.at[slot, part or 0],
             device_id=target["-" if side else "+"], device_id_type=MESH,
         )
 
-    def sibling_copy(k):
+    def sibling_copy(k, part):
         gather = 0 if k % 4 == 0 else 1
         return pltpu.make_async_remote_copy(
-            src_ref=amp if k == 0 else gath.at[k, gather], dst_ref=gath.at[k, 1 - gather],
-            send_sem=sib_s.at[k], recv_sem=sib_r.at[k],
+            src_ref=rows_of(amp if k == 0 else place(k, gather), part), dst_ref=rows_of(place(k, gather, 1), part),
+            send_sem=sib_s.at[k, part or 0], recv_sem=sib_r.at[k, part or 0],
             device_id=target["core"], device_id_type=MESH,
         )
 
@@ -122,20 +145,21 @@
             gather_copy(g, side).start()
 
     def handle(g):
-        for side in (0, 1):
-            gather_copy(g, side).wait_recv()
-        for k in GROUPS[g]:
-            sibling_copy(k).start()
+        groups, slots, part = ARRIVALS[g]
+        for group in groups:
+            for side in (0, 1):
+                gather_copy(group, side).wait_recv()
+        for k in slots:
+            sibling_copy(k, part).start()
 
     def passed(g):
-        for k in PASSED[g]:
-            pltpu.make_async_remote_copy(
-                src_ref=gath.at[k, 1], dst_ref=gath.at[k, 1], send_sem=sib_s.at[k], recv_sem=sib_r.at[k],
-                device_id=target["core"], device_id_type=MESH,
-            ).wait_recv()
+        slots, part = PASSED[g]
+        for k in slots:
+            sibling_copy(k, part).wait_recv()
 
     issue(0)
-    sibling_copy(0).start()
+    issue(1)
+    sibling_copy(0, None).start()
 
     column = index * ab_local + lax.broadcasted_iota(jnp.int32, (1, ab_local), 1)
 
@@ -158,7 +182,11 @@
     lax.fori_loop(0, tile_count, mask_tile, 0)
     amp_copy.wait()
 
-    def unit_place(u):
+    def unit_of(i):
+        return jnp.where(c == 0, pick(UNITS[0], 5, i), pick(UNITS[1], 5, i))
+
+    def unit_place(i):
+        u = unit_of(i)
         net = u // 16
         dp = (u % 16) // 4
         dq = u % 4
@@ -257,29 +285,30 @@
                     resbuf[slot, :, cols] = resbuf[slot, :, cols] + tiles_of(arrived, unit, j, scales)
             out_copy(slot).start()
 
-    def product(first, second):
-        for u in (first, second):
+    def product(p):
+        for i in (2 * p, 2 * p + 1):
+            u = unit_of(i)
 
             @pl.when(jnp.logical_and(u < 16, u % 4 != 0))
             def _():
                 pltpu.make_async_remote_copy(
-                    src_ref=gath.at[u, 0], dst_ref=gath.at[u, 0], send_sem=sib_s.at[u], recv_sem=sib_r.at[u],
+                    src_ref=gath.at[i], dst_ref=gath.at[i], send_sem=sib_s.at[u, 0], recv_sem=sib_r.at[u, 0],
                     device_id=target["core"], device_id_type=MESH,
                 ).wait_recv()
 
-        left = jnp.concatenate([gath[u % 16, u // 16] for u in (first, second)], axis=0)
+        left = gath[pl.ds(2 * p, 2)].reshape(2 * unit, cd_local)
         acc[...] = jnp.dot(left, right[...], preferred_element_type=jnp.float32)
-        after_product(first, 0)
-        after_product(second, 1)
+        after_product(2 * p, 0)
+        after_product(2 * p + 1, 1)
 
     def act(a, carry):
-        code = jnp.where(c == 0, pick(ACTIONS[0], a), pick(ACTIONS[1], a))
-        kind = code % 8
-        arg = (code // 8) % 32
+        code = jnp.where(c == 0, pick(ACTIONS[0], 8, a), pick(ACTIONS[1], 8, a))
+        kind = code & 7
+        arg = code >> 3
 
         @pl.when(kind == 0)
         def _():
-            product(arg, code // 256)
+            product(arg)
 
         @pl.when(kind == 1)
         def _():
@@ -289,7 +318,7 @@
         def _():
             own_stage(arg)
 
-        for this, count, do in ((3, len(GROUPS), handle), (4, len(GROUPS), issue), (5, len(PASSED), passed)):
+        for this, count, do in ((3, len(ARRIVALS), handle), (4, len(COPIES), issue), (5, len(PASSED), passed)):
 
             @pl.when(kind == this)
             def _():
@@ -303,11 +332,12 @@
 
     lax.fori_loop(0, len(ACTIONS[0]), act, 0)
 
-    for g in range(len(GROUPS)):
+    for g in range(len(COPIES)):
         for side in (0, 1):
             gather_copy(g, side).wait_send()
     for k in range(STEPS):
-        sibling_copy(k).wait_send()
+        for part in (0, 1) if k in (4, 12) else (None,):
+            sibling_copy(k, part).wait_send()
 
     def finish(slot, carry):
         for side in (0, 1):
@@ -342,7 +372,7 @@
         in_specs=[pl.BlockSpec(memory_space=pltpu.SMEM)] * 2 + [pl.BlockSpec(memory_space=pl.ANY)] * 2,
         out_specs=pl.BlockSpec(memory_space=pl.ANY),
         scratch_shapes=[
-            pltpu.VMEM((STEPS, 2, unit, cd_local), jnp.bfloat16),
+            pltpu.VMEM((2 * STEPS, unit, cd_local), jnp.bfloat16),
             pltpu.VMEM((cd_local, ab_local), jnp.bfloat16),
             pltpu.VMEM((2 * unit, ab_local), jnp.float32),
             pltpu.VMEM((2, 8, unit, ab_local), jnp.float32),
@@ -351,7 +381,7 @@
             pltpu.VMEM((2, 8, far, 16, LANES), jnp.int16),
             pltpu.VMEM((2, 8, near, 16, LANES), jnp.int16),
             pltpu.VMEM((2, 8, near, 16, LANES), jnp.int16),
-            dma, dma((cd_local // TCD,)), dma((8,)), dma((10, 2)), dma((STEPS, 2)), dma((STEPS,)), dma((STEPS,)),
+            dma, dma((cd_local // TCD,)), dma((8,)), dma((len(COPIES), 2)), dma((STEPS, 2)), dma((STEPS, 2)), dma((STEPS, 2)),
             dma((2, 8)), dma((2, 8)), dma((2, 8)), dma((2, 8)),
         ],
         compiler_params=pltpu.CompilerParams(

time: 82.4 us -> 82.3 us (level)
  no operation moved by 1% of the time
where the time goes in v4:
time: 82.3 us; the launch traced here: 81.7 us
  Pallas kernels  81.1 us (99%)
    pallas_call x1, Pallas kernels, body(): pl.pallas_call(kernel, out_shape=jax.ShapeDtypeStruct((rows, ab_local), j...  77.2 us
    pallas_call x1, Pallas kernels, body(): pl.pallas_call(divide, grid=(rows // 256,), out_shape=(jax.ShapeDtypeStru...  3.89 us

profile of v4, /device:TPU:18, one launch (start us, length us, event | category | flops | bytes accessed | tf_op | source)
XLA Modules:
  0.0 81.7 jit_solution(10907685353892677813)
XLA Ops:
  0.6 77.2 %shard_map.77.sums = f32[512,1280]{1,0:T(8,128)} custom-call(s32[8]{0:T(128)} %ab_sizes.1, s32[8]{0:T(128)} %cd_sizes.1, bf16[64,4096]{1,0:T(8,128)(2,1)} %amp.1, bf16[4096,1280]{1,0:T(8,128)(2,1)} %integ.1), custom_call_target="tpu_custom_call" | custom-call | tf_op jit(solution)/shard_map/pallas_call | solution.py:369
  77.8 3.9 %shard_map.78 = (f32[512,1280]{1,0:T(8,128)}, f32[512,1280]{1,0:T(8,128)}) custom-call(f32[512,1280]{1,0:T(8,128)} %shard_map.77.sums, f32[1280]{0:T(1024)} %virt.1, f32[512]{0:T(512)} %occ.1), custom_call_target="tpu_custom_call" | custom-call | tf_op jit(solution)/shard_map/pallas_call | solution.py:392

commit v5 on v4

--- a/solution.py
+++ b/solution.py
@@ -28,28 +28,28 @@
 
 UNITS = (
     (
-        0, 16, 4, 12, 20, 28, 8, 1, 3, 24, 21, 23, 13, 29, 31, 15, 2, 14, 25, 27, 5, 17, 19, 7, 26, 9,
-        11, 22, 6, 30, 10, 18,
+        0, 16, 4, 12, 20, 28, 8, 24, 29, 31, 13, 15, 25, 27, 5, 7, 14, 21, 23, 6, 17, 19, 1, 26, 3, 22,
+        9, 18, 11, 30, 2, 10,
     ),
     (
-        0, 16, 4, 12, 20, 28, 17, 19, 24, 8, 29, 31, 5, 7, 18, 30, 13, 15, 21, 23, 9, 11, 1, 25, 27, 3,
-        10, 22, 26, 6, 14, 2,
+        0, 16, 4, 12, 20, 28, 8, 24, 29, 31, 13, 15, 21, 23, 9, 30, 11, 22, 5, 7, 17, 19, 1, 3, 10, 25,
+        27, 6, 18, 2, 26, 14,
     ),
 )
 ACTIONS = (
     (
-        5, 0, 3, 11, 20, 8, 1, 9, 13, 21, 36, 44, 60, 68, 16, 17, 19, 2, 24, 10, 29, 52, 28, 25, 35, 33,
-        32, 41, 40, 49, 18, 73, 51, 48, 57, 56, 26, 34, 65, 64, 43, 92, 84, 100, 81, 89, 72, 58, 74, 50, 42, 105,
-        66, 113, 27, 76, 80, 129, 121, 88, 137, 97, 75, 82, 96, 67, 169, 161, 145, 153, 130, 104, 83, 185, 112, 59, 201, 146,
-        120, 177, 90, 106, 138, 114, 209, 217, 170, 122, 98, 154, 193, 178, 233, 162, 249, 194, 186, 225, 202, 250, 241, 210, 218, 226,
-        234, 242,
+        5, 0, 3, 11, 20, 8, 1, 9, 13, 21, 60, 68, 16, 17, 19, 25, 2, 29, 52, 36, 44, 28, 24, 10, 33, 51,
+        32, 41, 18, 57, 49, 40, 34, 26, 43, 92, 48, 42, 56, 65, 58, 97, 35, 84, 64, 73, 105, 72, 81, 113, 89, 50,
+        27, 76, 100, 80, 137, 98, 121, 66, 106, 75, 88, 129, 145, 67, 96, 153, 161, 169, 74, 82, 59, 104, 114, 90, 138, 83,
+        112, 177, 193, 130, 122, 146, 162, 120, 201, 185, 225, 233, 217, 170, 154, 209, 194, 178, 241, 186, 249, 218, 202, 226, 242, 234,
+        210, 250,
     ),
     (
-        5, 28, 0, 3, 11, 20, 8, 1, 13, 21, 60, 68, 16, 9, 17, 27, 25, 76, 24, 29, 19, 32, 33, 41, 2, 18,
-        26, 51, 100, 36, 44, 52, 40, 65, 57, 73, 49, 59, 48, 83, 56, 64, 10, 74, 34, 58, 42, 81, 113, 89, 50, 35,
-        84, 72, 121, 80, 97, 66, 105, 129, 114, 137, 43, 92, 88, 145, 96, 67, 153, 104, 75, 161, 169, 90, 122, 112, 185, 193,
-        130, 98, 177, 106, 120, 201, 146, 162, 82, 178, 154, 209, 138, 217, 225, 170, 233, 241, 202, 249, 250, 242, 186, 194, 226, 234,
-        210, 218,
+        5, 0, 3, 11, 20, 8, 1, 13, 21, 60, 68, 36, 44, 16, 9, 17, 19, 25, 29, 24, 33, 41, 2, 18, 26, 51,
+        100, 32, 49, 57, 40, 10, 35, 84, 28, 52, 48, 34, 83, 56, 65, 73, 42, 50, 67, 64, 58, 113, 97, 72, 121, 27,
+        76, 80, 81, 89, 105, 129, 66, 137, 88, 74, 145, 114, 43, 92, 96, 169, 98, 104, 59, 122, 153, 161, 82, 130, 112, 75,
+        138, 90, 120, 177, 185, 209, 146, 106, 201, 193, 154, 170, 162, 249, 217, 225, 233, 178, 241, 186, 226, 210, 194, 202, 234, 242,
+        218, 250,
     ),
 )
 PLACE = tuple({u: i for i, u in enumerate(units)} for units in UNITS)

time: 82.3 us -> 84 us (1.021)
  Pallas kernels: 81.1 us -> 83 us
    pallas_call x1, Pallas kernels: 77.2 us -> 79.1 us  [body(): pl.pallas_call(kernel, out_shape=jax.ShapeDtypeStruct((rows, ab_local), j...]
where the time goes in v5:
time: 84 us; the launch traced here: 83.6 us
  Pallas kernels  83 us (99%)
    pallas_call x1, Pallas kernels, body(): pl.pallas_call(kernel, out_shape=jax.ShapeDtypeStruct((rows, ab_local), j...  79.1 us
    pallas_call x1, Pallas kernels, body(): pl.pallas_call(divide, grid=(rows // 256,), out_shape=(jax.ShapeDtypeStru...  3.89 us

profile of v5, /device:TPU:18, one launch (start us, length us, event | category | flops | bytes accessed | tf_op | source)
XLA Modules:
  0.0 83.6 jit_solution(15949915997114250896)
XLA Ops:
  0.6 79.1 %shard_map.77.sums = f32[512,1280]{1,0:T(8,128)} custom-call(s32[8]{0:T(128)} %ab_sizes.1, s32[8]{0:T(128)} %cd_sizes.1, bf16[64,4096]{1,0:T(8,128)(2,1)} %amp.1, bf16[4096,1280]{1,0:T(8,128)(2,1)} %integ.1), custom_call_target="tpu_custom_call" | custom-call | tf_op jit(solution)/shard_map/pallas_call | solution.py:369
  79.7 3.9 %shard_map.78 = (f32[512,1280]{1,0:T(8,128)}, f32[512,1280]{1,0:T(8,128)}) custom-call(f32[512,1280]{1,0:T(8,128)} %shard_map.77.sums, f32[1280]{0:T(1024)} %virt.1, f32[512]{0:T(512)} %occ.1), custom_call_target="tpu_custom_call" | custom-call | tf_op jit(solution)/shard_map/pallas_call | solution.py:392
